TPU v7x, 256 devices: a whole 4x4x8 slice. The times are simulated.
256 devices in a mesh: ctx: 16 (over x_hi, z), head: 8 (over y, core), pair: 2 (over x_lo).
Axes of the slice: x: 4 (x_hi: 2, x_lo: 2; x = x_hi * 2 + x_lo), y: 4, z: 8, core: 2. Of those that a mesh axis runs over, the one named last changes fastest.
Arguments:
- queries: bfloat16 [2048, 64, 128], P(('pair', 'ctx'), 'head'), parts along dimension 0, may hold values from -6 to 6
- keys: bfloat16 [65536, 8, 128], P(('pair', 'ctx'), 'head'), parts along dimension 0, may hold values from -6 to 6
- values: bfloat16 [65536, 8, 128], P(('pair', 'ctx'), 'head'), parts along dimension 0, may hold values from -6 to 6
- lengths: int32 [4], P('pair'), parts along dimension 0, may hold values from 256 to 512, as said below
- prompt_lengths: int32 [2], P('pair'), parts along dimension 0, may hold values from 16384 to 32768
- out_weight: bfloat16 [8192, 8192], P('head', 'ctx'), may hold values from -0.0625 to 0.0625
Outputs:
- projected: float32 [2048, 8192], P(('pair', 'head'), 'ctx'), parts along dimension 0
There are 2 independent parts, one for each index of `pair`. A program takes and returns all parts, laid end to end along the dimension named above; an argument that names none is the same for every part. Nothing has to cross between parts.
Inputs may be any that keep to these rules, and one draw needn't show every extreme that they name: `lengths`: one of the two responses has exactly 512 real tokens, the other at least 256.
All inputs are finite; a program needn't handle non-finite values.
Results may differ from a plain program's by a relative error of at most 0.013.
Values may be sent and summed in bfloat16 or wider, within the bound.
A program may use at most 64 MiB of HBM per device.

v0:
```python
import jax
import jax.numpy as jnp
from jax import lax
from jax.experimental import pallas as pl
from jax.experimental.pallas import tpu as pltpu
from jax.sharding import PartitionSpec as P

MESH = pl.DeviceIdType.MESH
F32 = jnp.float32
BF16 = jnp.bfloat16
NT = (((1,), (1,)), ((), ()))
NN = (((1,), (0,)), ((), ()))
HIDDEN = -(2.0 ** 100)
LOG2E = 1.4426950408889634

TOKENS = 64
GROUP = 8
WIDTH = 128
ROWS = TOKENS * GROUP
SPAN = 1024
STRIP = 256
RING = 8
FEATURES = GROUP * WIDTH
COLUMNS = 512
SCALE = WIDTH ** -0.5 * LOG2E
HALF = ROWS // 2
PIECES = 4
LANES = ROWS // PIECES
PART = TOKENS // PIECES
LATE = 10


def rising(slot, piece):
    return slot % 2 == 1 if slot < 7 else piece % 2 == 0


def before(slot, piece):
    if slot == 7:
        return 5 if piece % 2 == 0 else 6
    return max(slot - 2, 0)


def long_way(piece):
    return (7, 5, 3, 1) if piece % 2 == 0 else (7, 6, 4, 2)


def short_way(piece):
    return (6, 4, 2) if piece % 2 == 0 else (5, 3, 1)


def kernel(
    q_ref, k_ref, v_ref, len_ref, plen_ref, w_ref, out_ref,
    v_in, w_all, q_all, k_all, vt_all, score, peak, acc, top,
    go, come, turn, mixed, part, mate_in, y_out, y_in, own,
    in_sem, kv_send, kv_recv, q_send, q_recv, rs_send, rs_recv,
    w_send, w_recv, ag_send, ag_recv, co_send, co_recv, y_send, y_recv,
):
    ctx = lax.axis_index("ctx")
    head = lax.axis_index("head")
    side, z = ctx // RING, ctx % RING
    y, core = head // 2, head % 2

    def z_at(step):
        return {"ctx": side * RING + (z + step + RING) % RING}

    def y_at(to):
        return {"head": to * 2 + core}

    partner = {"ctx": (1 - side) * RING + z}
    mate = {"head": y * 2 + 1 - core}

    def opposite(to):
        return {"ctx": (1 - side) * RING + z, "head": to * 2 + core}

    def remote(src, dst, send, recv, to):
        return pltpu.make_async_remote_copy(
            src_ref=src, dst_ref=dst, send_sem=send, recv_sem=recv,
            device_id=to, device_id_type=MESH,
        )

    barrier = pltpu.get_barrier_semaphore()
    met = [z_at(1), z_at(-1), mate] + [y_at((y + step) % 4) for step in range(1, 4)] + [opposite(to) for to in range(4)]
    for to in met:
        pl.semaphore_signal(barrier, inc=1, device_id=to, device_id_type=MESH)

    loads = [
        pltpu.make_async_copy(k_ref.at[pl.ds(chunk * SPAN, SPAN)], k_all.at[chunk], in_sem.at[chunk]) for chunk in range(2)
    ]
    v_load = pltpu.make_async_copy(v_ref, v_in, in_sem.at[2])
    q_load = pltpu.make_async_copy(q_ref, q_all.at[0], in_sem.at[3])
    w_load = pltpu.make_async_copy(w_ref, w_all.at[side], in_sem.at[4])
    for load in (v_load, *loads, q_load, w_load):
        load.start()

    plen = plen_ref[0]

    def chunk_start(chunk):
        holder = jnp.where(chunk < 2, side, 1 - side)
        return (holder * RING + z) * 2 * SPAN + (chunk % 2) * SPAN

    def seen_rows(chunk):
        return chunk_start(chunk) + lax.broadcasted_iota(jnp.int32, (SPAN, WIDTH), 0) < plen

    def hide_keys(chunk):
        keys = k_all[chunk].astype(F32)
        k_all[chunk] = jnp.where(seen_rows(chunk), keys, keys[0:1, :]).astype(BF16)

    def turn_values(chunk):
        vals = jnp.where(seen_rows(chunk), v_in[pl.ds(chunk * SPAN, SPAN), :].astype(F32), 0.0)
        vt_all[chunk, 0:WIDTH, :] = vals.T.astype(BF16)

    def q_copy(n, half, slot):
        to = jnp.where(slot % 2 == 1, 1, -1)
        rows = pl.ds(half * HALF, HALF)
        src = q_ref.at[rows] if n is None else q_all.at[n, rows]
        return remote(src, q_all.at[slot, rows], q_send.at[slot * 2 + half], q_recv.at[slot * 2 + half], z_at(to))

    def kv_copy(index):
        chunk = index // 2
        if index % 2 == 0:
            src, dst = k_ref.at[pl.ds(chunk * SPAN, SPAN)], k_all.at[chunk + 2]
        else:
            src, dst = vt_all.at[chunk, 0:WIDTH], vt_all.at[chunk + 2, 0:WIDTH]
        return remote(src, dst, kv_send.at[index], kv_recv.at[index], partner)

    w_copy = remote(w_ref, w_all.at[side], w_send, w_recv, partner)

    acc[...] = jnp.zeros_like(acc)
    top[...] = jnp.full_like(top, HIDDEN)
    for chunk in range(4):
        seen = chunk_start(chunk) + lax.broadcasted_iota(jnp.int32, (16, SPAN), 1) < plen
        vt_all[chunk, WIDTH:, :] = jnp.where(seen, 1.0, 0.0).astype(BF16)

    pl.semaphore_wait(barrier, len(met))
    kv_copy(0).start()
    for half in range(2):
        for slot in (1, 2):
            q_copy(None, half, slot).start()
    v_load.wait()
    turn_values(0)
    kv_copy(1).start()
    turn_values(1)
    for chunk in range(2):
        loads[chunk].wait()
        hide_keys(chunk)
    q_load.wait()

    def task(t):
        n = jnp.where(t < 16, t // 2, jnp.where(t < 24, t - 16, 31 - t))
        chunk = jnp.where(t < 16, t % 2, jnp.where(t < 24, 2, 3))
        return n, chunk

    def ready(t):
        @pl.when(jnp.logical_and(jnp.logical_and(t >= 2, t < 16), t % 2 == 0))
        def _():
            n = t // 2
            for half in range(2):
                q_copy(None, half, n).wait_recv()

                @pl.when(n + 2 < RING)
                def _():
                    q_copy(n, half, n + 2).start()

        @pl.when(t == LATE)
        def _():
            kv_copy(2).start()
            kv_copy(3).start()

        @pl.when(t == 16)
        def _():
            kv_copy(0).wait_recv()
            hide_keys(2)

        @pl.when(t == 24)
        def _():
            kv_copy(2).wait_recv()
            hide_keys(3)

    def ready_values(t):
        @pl.when(t == 16)
        def _():
            kv_copy(1).wait_recv()

        @pl.when(t == 24)
        def _():
            kv_copy(3).wait_recv()
            w_copy.start()

    def step(ahead, slot_ahead, now, slot_now):
        if ahead is not None:
            n_ahead, c_ahead = task(ahead)
            queries = q_all[n_ahead]
        if now is not None:
            n_now, c_now = task(now)
            best = peak[slot_now, 0:1, :]
        total = highest = None
        for strip in range(0, SPAN, STRIP):
            at = pl.ds(strip, STRIP)
            if ahead is not None:
                s = lax.dot_general(k_all[c_ahead, at, :], queries, NT, preferred_element_type=F32)
                score[slot_ahead, at, :] = s
                high = jnp.max(s.reshape(STRIP // 8, 8, ROWS), axis=0)
                highest = high if highest is None else jnp.maximum(highest, high)
            if now is not None:
                weights = jnp.exp2((score[slot_now, at, :] - best) * SCALE).astype(BF16)
                term = lax.dot_general(vt_all[c_now, :, at], weights, NN, preferred_element_type=F32)
                total = term if total is None else total + term
        if ahead is not None:
            peak[slot_ahead, 0:1, :] = jnp.max(highest, axis=0, keepdims=True).astype(BF16).astype(F32)
        if now is not None:
            best = jnp.where(chunk_start(c_now) < plen, best, HIDDEN)
            old = top[n_now, 0:1, :]
            new = jnp.maximum(old, best)
            top[n_now, 0:1, :] = new
            acc[n_now] = acc[n_now] * jnp.exp2((old - new) * SCALE) + total[0:136] * jnp.exp2((best - new) * SCALE)

    def rs_copy(slot, piece):
        i = slot * PIECES + piece
        to = -1 if rising(slot, piece) else 1
        return remote(go.at[i], come.at[i], rs_send.at[i], rs_recv.at[i], z_at(to))

    def mine(slot, piece):
        lanes = pl.ds(piece * LANES, LANES)
        return acc[slot, 0:WIDTH, lanes], acc[slot, WIDTH:WIDTH + 1, lanes], top[slot, 0:1, lanes]

    def joined(state, piece, source):
        rs_copy(source, piece).wait_recv()
        sums, total, old = state
        i = source * PIECES + piece
        stats = come[i, WIDTH:, :].astype(F32)
        best = stats[0:1]
        new = jnp.maximum(old, best)
        keep, add = jnp.exp2((old - new) * SCALE), jnp.exp2((best - new) * SCALE)
        return sums * keep + come[i, 0:WIDTH, :].astype(F32) * add, total * keep + (stats[1:2] + stats[2:3]) * add, new

    def pass_on(slot, piece, state):
        sums, total, best = state
        i = slot * PIECES + piece
        go[i, 0:WIDTH, :] = sums.astype(BF16)
        high = total.astype(BF16).astype(F32)
        row = lax.broadcasted_iota(jnp.int32, (16, LANES), 0)
        stats = jnp.where(row == 0, best, jnp.where(row == 1, high, jnp.where(row == 2, total - high, 0.0)))
        go[i, WIDTH:, :] = stats.astype(BF16)
        rs_copy(slot, piece).start()

    def relay(way, level, piece):
        pass_on(way[level], piece, joined(mine(way[level], piece), piece, way[level - 1]))

    def relay_long(level):
        for piece in range(PIECES):
            relay(long_way(piece), level, piece)

    def relay_short(level):
        for piece in (1, 0, 3, 2):
            relay(short_way(piece), level, piece)

    def returns(t):
        @pl.when(t == 24)
        def _():
            for piece in range(PIECES):
                pass_on(7, piece, mine(7, piece))

        @pl.when(t == 25)
        def _():
            for piece in range(0, PIECES, 2):
                pass_on(6, piece, mine(6, piece))

        @pl.when(t == 26)
        def _():
            for piece in range(1, PIECES, 2):
                pass_on(5, piece, mine(5, piece))

        @pl.when(t == 28)
        def _():
            relay_long(1)

        @pl.when(t == 29)
        def _():
            relay_short(1)

    ready(0)
    step(0, 0, None, None)

    def two(g, _):
        t = g * 2
        ready(t + 1)
        ready_values(t)
        step(t + 1, 1, t, 0)
        returns(t)
        ready(t + 2)
        step(jnp.minimum(t + 2, 31), 0, t + 1, 1)
        returns(t + 1)
        return 0

    lax.fori_loop(0, 16, two, 0)

    relay_long(2)
    relay_short(2)
    relay_long(3)

    def ag_copy(slot, piece):
        i = slot * PIECES + piece
        rows = pl.ds(piece * PART, PART)
        to = 1 if rising(slot, piece) else -1
        return remote(mixed.at[before(slot, piece), rows], mixed.at[slot, rows], ag_send.at[i], ag_recv.at[i], z_at(to))

    def finish(piece):
        state = joined(mine(0, piece), piece, short_way(piece)[2])
        sums, total, _ = joined(state, piece, long_way(piece)[3])
        token = piece * PART + lax.broadcasted_iota(jnp.int32, (1, LANES), 1) // GROUP
        live = z * TOKENS + token < jnp.where(side == 0, len_ref[0], len_ref[1])
        done = jnp.where(live, sums / total, 0.0)
        turn[piece] = done.T
        for j in range(GROUP):
            mixed[0, pl.ds(piece * PART, PART), j * WIDTH:(j + 1) * WIDTH] = turn[piece, pl.ds(j, PART, stride=GROUP), :].astype(BF16)
        ag_copy(1, piece).start()
        ag_copy(2, piece).start()

    def arrive(*slots):
        for piece in range(PIECES):
            for slot in slots:
                ag_copy(slot, piece).wait_recv()
                for later in range(3, RING):
                    if before(later, piece) == slot:
                        ag_copy(later, piece).start()

    def chip_of(slot):
        return (z + (-((slot + 1) // 2) if slot % 2 == 1 else slot // 2) + RING) % RING

    def to_mate(slot, block):
        i = slot * 2 + block
        return remote(part.at[slot, block], mate_in.at[slot, block], co_send.at[i], co_recv.at[i], mate)

    def given(slot):
        return (chip_of(slot) // 2) % 2 != core

    def project(block, first, last):
        rows = mixed[first:last].reshape((last - first) * TOKENS, FEATURES)
        terms = jnp.dot(rows, w_all[block], preferred_element_type=F32)
        part[first:last, block] = terms.reshape(last - first, TOKENS, COLUMNS)

        for slot in range(first, last):
            @pl.when(given(slot))
            def _():
                to_mate(slot, block).start()

    def y_copy(block, far, which):
        i = (block * 2 + far) * 2 + which
        to = {"ctx": block * RING + z, "head": (2 * side + far) * 2 + core}
        return remote(y_out.at[i], y_in.at[y * 2 + which], y_send.at[i], y_recv.at[y * 2 + which], to)

    def stays(block, far):
        return jnp.logical_and(block == side, 2 * side + far == y)

    def spread(block, first, last):
        for slot in range(first, last):
            at = chip_of(slot)
            far, which = at // 4, at % 2

            @pl.when(jnp.logical_not(given(slot)))
            def _():
                to_mate(slot, block).wait_recv()
                both = part[slot, block] + mate_in[slot, block]

                @pl.when(stays(block, far))
                def _():
                    own[which] = both

                @pl.when(jnp.logical_not(stays(block, far)))
                def _():
                    y_out[(block * 2 + far) * 2 + which] = both.astype(BF16)
                    y_copy(block, far, which).start()

    there = 1 - side
    for piece in (1, 0, 2, 3):
        finish(piece)
    w_load.wait()
    arrive(1, 2)
    project(side, 0, 1)
    arrive(3, 4)
    project(side, 1, 3)
    spread(side, 0, 1)
    arrive(5, 6)
    project(side, 3, 5)
    spread(side, 1, 3)
    w_copy.wait_recv()
    project(there, 0, 5)
    project(side, 5, 7)
    spread(there, 0, 5)
    project(there, 5, 7)
    spread(side, 3, 7)
    spread(there, 5, 7)
    arrive(7)
    project(there, 7, 8)
    project(side, 7, 8)
    spread(there, 7, 8)
    spread(side, 7, 8)

    def taken(source, which):
        i = source * 2 + which
        remote(y_out.at[which], y_in.at[i], y_send.at[which], y_recv.at[i], opposite(source)).wait_recv()
        return y_in[i].astype(F32)

    for which in range(2):
        rows = pl.ds(which * TOKENS, TOKENS)

        @pl.when(y // 2 == side)
        def _():
            out_ref[rows, :] = own[which] + taken((y + 1) % 4, which) + taken((y + 2) % 4, which) + taken((y + 3) % 4, which)

        @pl.when(y // 2 != side)
        def _():
            out_ref[rows, :] = taken(0, which) + taken(1, which) + taken(2, which) + taken(3, which)

    for index in range(4):
        kv_copy(index).wait_send()
    for slot in range(1, RING):
        for half in range(2):
            q_copy(None, half, slot).wait_send()
        for piece in range(PIECES):
            rs_copy(slot, piece).wait_send()
            ag_copy(slot, piece).wait_send()
    w_copy.wait_send()
    for slot in range(RING):
        @pl.when(given(slot))
        def _():
            for block in range(2):
                to_mate(slot, block).wait_send()
    for block in range(2):
        for far in range(2):
            for which in range(2):
                @pl.when(jnp.logical_not(stays(block, far)))
                def _():
                    y_copy(block, far, which).wait_send()


def body(queries, keys, values, lengths, prompt_lengths, out_weight):
    hbm = pl.BlockSpec(memory_space=pltpu.HBM)
    smem = pl.BlockSpec(memory_space=pltpu.SMEM)
    dma = pltpu.SemaphoreType.DMA
    return pl.pallas_call(
        kernel,
        out_shape=jax.ShapeDtypeStruct((2 * TOKENS, COLUMNS), F32),
        in_specs=[hbm, hbm, hbm, smem, smem, hbm],
        out_specs=pl.BlockSpec(memory_space=pltpu.VMEM),
        scratch_shapes=[
            pltpu.VMEM((2 * SPAN, WIDTH), BF16),
            pltpu.VMEM((2, FEATURES, COLUMNS), BF16),
            pltpu.VMEM((RING, ROWS, WIDTH), BF16),
            pltpu.VMEM((4, SPAN, WIDTH), BF16),
            pltpu.VMEM((4, WIDTH + 16, SPAN), BF16),
            pltpu.VMEM((2, SPAN, ROWS), F32),
            pltpu.VMEM((2, 8, ROWS), F32),
            pltpu.VMEM((RING, WIDTH + 8, ROWS), F32),
            pltpu.VMEM((RING, 8, ROWS), F32),
            pltpu.VMEM((RING * PIECES, WIDTH + 16, LANES), BF16),
            pltpu.VMEM((RING * PIECES, WIDTH + 16, LANES), BF16),
            pltpu.VMEM((PIECES, LANES, WIDTH), F32),
            pltpu.VMEM((RING, TOKENS, FEATURES), BF16),
            pltpu.VMEM((RING, 2, TOKENS, COLUMNS), F32),
            pltpu.VMEM((RING, 2, TOKENS, COLUMNS), F32),
            pltpu.VMEM((8, TOKENS, COLUMNS), BF16),
            pltpu.VMEM((8, TOKENS, COLUMNS), BF16),
            pltpu.VMEM((2, TOKENS, COLUMNS), F32),
            dma((5,)),
            dma((4,)), dma((4,)),
            dma((2 * RING,)), dma((2 * RING,)),
            dma((RING * PIECES,)), dma((RING * PIECES,)),
            dma, dma,
            dma((RING * PIECES,)), dma((RING * PIECES,)),
            dma((2 * RING,)), dma((2 * RING,)),
            dma((8,)), dma((8,)),
        ],
        compiler_params=pltpu.CompilerParams(
            collective_id=1, has_side_effects=True, vmem_limit_bytes=56 << 20
        ),
        name="paired_attention",
    )(
        queries.reshape(ROWS, WIDTH),
        keys.reshape(2 * SPAN, WIDTH),
        values.reshape(2 * SPAN, WIDTH),
        lengths,
        prompt_lengths,
        out_weight,
    )


def solution(mesh):
    in_specs = (
        P(("pair", "ctx"), "head", None),
        P(("pair", "ctx"), "head", None),
        P(("pair", "ctx"), "head", None),
        P("pair"),
        P("pair"),
        P("head", "ctx"),
    )
    out_specs = P(("pair", "head"), "ctx")
    return jax.shard_map(body, mesh=mesh, in_specs=in_specs, out_specs=out_specs, check_vma=False)
```

profile of v0, /device:TPU:7, one launch (start us, length us, event | category | flops | bytes accessed | tf_op | source)
XLA Modules:
  0.0 79.4 jit_solution(18239754543722614794)
XLA Ops:
  0.7 77.1 %paired_attention.1 = f32[128,512]{1,0:T(8,128)} custom-call(bf16[512,128]{1,0:T(8,128)(2,1)} %bitcast.5, bf16[2048,128]{1,0:T(8,128)(2,1)} %bitcast.3, bf16[2048,128]{1,0:T(8,128)(2,1)} %bitcast.4, s32[2]{0:T(128)} %len_ref.1, s32[1]{0:T(128)S(6)} %copy.8.plen_ref, bf16[1024,512]{1,0:T(8,128)(2,1)} %w_ref.1), custom_call_target="tpu_custom_call" | custom-call | tf_op jit(solution)/shard_map/paired_attention/pallas_call | solution.py:441
  77.7 1.7 %copy.9 = f32[128,512]{1,0:T(8,128)} copy(f32[128,512]{1,0:T(8,128)} %paired_attention.1) | data formatting | bytes 524288
where the time goes:
time: 79.5 us; the launch traced here: 79.4 us
  Pallas kernels  77.1 us (97%)
  local copies, waits for them, and re-layouts  1.67 us (2%)
    pallas_call x1, Pallas kernels, body(): pl.pallas_call(kernel, out_shape=jax.ShapeDtypeStruct((2 * TOKENS, COLUMN...  77.1 us
    unnamed x1, local copies, waits for them, and re-layouts  1.67 us

commit v1 on v0

--- a/solution.py
+++ b/solution.py
@@ -372,17 +372,15 @@
                     y_copy(block, far, which).start()
 
     there = 1 - side
-    for piece in (1, 0, 2, 3):
+    for piece in range(PIECES):
         finish(piece)
     w_load.wait()
     arrive(1, 2)
-    project(side, 0, 1)
     arrive(3, 4)
-    project(side, 1, 3)
-    spread(side, 0, 1)
+    project(side, 0, 3)
     arrive(5, 6)
     project(side, 3, 5)
-    spread(side, 1, 3)
+    spread(side, 0, 3)
     w_copy.wait_recv()
     project(there, 0, 5)
     project(side, 5, 7)
@@ -440,7 +438,7 @@
     dma = pltpu.SemaphoreType.DMA
     return pl.pallas_call(
         kernel,
-        out_shape=jax.ShapeDtypeStruct((2 * TOKENS, COLUMNS), F32),
+        out_shape=pltpu.VMEM((2 * TOKENS, COLUMNS), F32),
         in_specs=[hbm, hbm, hbm, smem, smem, hbm],
         out_specs=pl.BlockSpec(memory_space=pltpu.VMEM),
         scratch_shapes=[

time: 79.5 us -> 77.2 us (0.971)
  Pallas kernels: 77.1 us -> 75.8 us
  local copies, waits for them, and re-layouts: 1.67 us -> 0.71 us
    pallas_call x1, Pallas kernels: 77.1 us -> 75.8 us  [body(): pl.pallas_call(kernel, out_shape=pltpu.VMEM((2 * TOKENS, COLUMNS), F32),...]
    unnamed x1, local copies, waits for them, and re-layouts: 1.67 us -> 0.71 us
where the time goes in v1:
time: 77.2 us; the launch traced here: 77.1 us
  Pallas kernels  75.8 us (98%)
    pallas_call x1, Pallas kernels, body(): pl.pallas_call(kernel, out_shape=pltpu.VMEM((2 * TOKENS, COLUMNS), F32),...  75.8 us

profile of v1, /device:TPU:7, one launch (start us, length us, event | category | flops | bytes accessed | tf_op | source)
XLA Modules:
  0.0 77.1 jit_solution(6417124571876392657)
XLA Ops:
  0.7 75.8 %paired_attention.1 = f32[128,512]{1,0:T(8,128)S(1)} custom-call(bf16[512,128]{1,0:T(8,128)(2,1)} %bitcast.5, bf16[2048,128]{1,0:T(8,128)(2,1)} %bitcast.3, bf16[2048,128]{1,0:T(8,128)(2,1)} %bitcast.4, s32[2]{0:T(128)} %len_ref.1, s32[1]{0:T(128)S(6)} %copy.9.plen_ref, bf16[1024,512]{1,0:T(8,128)(2,1)} %w_ref.1), custom_call_target="tpu_custom_call" | custom-call | tf_op jit(solution)/shard_map/paired_attention/pallas_call | solution.py:439
  76.4 0.7 copy.8

commit v2 on v1

--- a/solution.py
+++ b/solution.py
@@ -304,8 +304,7 @@
         to = 1 if rising(slot, piece) else -1
         return remote(mixed.at[before(slot, piece), rows], mixed.at[slot, rows], ag_send.at[i], ag_recv.at[i], z_at(to))
 
-    def finish(piece):
-        state = joined(mine(0, piece), piece, short_way(piece)[2])
+    def finish(piece, state):
         sums, total, _ = joined(state, piece, long_way(piece)[3])
         token = piece * PART + lax.broadcasted_iota(jnp.int32, (1, LANES), 1) // GROUP
         live = z * TOKENS + token < jnp.where(side == 0, len_ref[0], len_ref[1])
@@ -372,8 +371,9 @@
                     y_copy(block, far, which).start()
 
     there = 1 - side
+    half_done = [joined(mine(0, piece), piece, short_way(piece)[2]) for piece in range(PIECES)]
     for piece in range(PIECES):
-        finish(piece)
+        finish(piece, half_done[piece])
     w_load.wait()
     arrive(1, 2)
     arrive(3, 4)

time: 77.2 us -> 77.2 us (level)
  no operation moved by 1% of the time
where the time goes in v2:
time: 77.2 us; the launch traced here: 77.1 us
  Pallas kernels  75.8 us (98%)
    pallas_call x1, Pallas kernels, body(): pl.pallas_call(kernel, out_shape=pltpu.VMEM((2 * TOKENS, COLUMNS), F32),...  75.8 us

profile of v2, /device:TPU:7, one launch (start us, length us, event | category | flops | bytes accessed | tf_op | source)
XLA Modules:
  0.0 77.1 jit_solution(4546542403193858137)
XLA Ops:
  0.7 75.8 %paired_attention.1 = f32[128,512]{1,0:T(8,128)S(1)} custom-call(bf16[512,128]{1,0:T(8,128)(2,1)} %bitcast.5, bf16[2048,128]{1,0:T(8,128)(2,1)} %bitcast.3, bf16[2048,128]{1,0:T(8,128)(2,1)} %bitcast.4, s32[2]{0:T(128)} %len_ref.1, s32[1]{0:T(128)S(6)} %copy.9.plen_ref, bf16[1024,512]{1,0:T(8,128)(2,1)} %w_ref.1), custom_call_target="tpu_custom_call" | custom-call | tf_op jit(solution)/shard_map/paired_attention/pallas_call | solution.py:439
  76.4 0.7 copy.8
